TPU v7x, 32 devices: a whole 2x2x4 slice. The times are simulated.
32 devices in a mesh: ctx: 8 (over z, y), head: 4 (over x, core).
Axes of the slice: x: 2, y: 2, z: 4, core: 2. Of those that a mesh axis runs over, the one named last changes fastest.
Arguments:
- ctx_queries: bfloat16 [8192, 4096], P('ctx', 'head'), may hold values from -8 to 8
- ctx_keys: bfloat16 [8192, 512], P('ctx', 'head'), may hold values from -12 to 12
- ctx_values: bfloat16 [8192, 512], P('ctx', 'head'), may hold values from -12 to 12
- new_queries: bfloat16 [64, 4096], P('ctx', 'head'), may hold values from -8 to 8
- out_weight: bfloat16 [4096, 8192], P('head', 'ctx'), may hold values from -0.09375 to 0.09375
- host_block: int32 [8], replicated, may hold values from 0 to 7, each once
- block_lengths: int32 [8], replicated, may hold values from 256 to 1024, as said below
Outputs:
- context_out: bfloat16 [8192, 4096], P('ctx', 'head')
- answer: bfloat16 [64, 8192], P('head', 'ctx')
Inputs may be any that keep to these rules, and one draw needn't show every extreme that they name: `block_lengths`: some block has 1024 valid tokens and another exactly 256. `host_block`: a permutation of the blocks.
All inputs are finite; a program needn't handle non-finite values.
Results may differ from a plain program's by a relative error of at most 0.002.
The roundings to bfloat16 on the way count: a program that leaves them out, or rounds other values in their place, can miss the bound.
Values may be sent and summed in bfloat16 or wider, within the bound.
No kernel may reach another device: no remote copies, remote signals or barrier semaphores. Data moves between devices by JAX's collectives and lax.ppermute only.
A program may use at most 128 MiB of HBM per device.

v0:
```python
import functools

import jax
import jax.numpy as jnp
from jax import lax
from jax.experimental import pallas as pl
from jax.experimental.pallas import tpu as pltpu
from jax.sharding import PartitionSpec as P

HD = 128
CLIP_FACTOR = 2.0
NEG = -1e30
LOG2E = 1.4426950408889634
NT = (((1,), (1,)), ((), ()))
SPREAD = 4
SPREAD_BITS = (1, 2)
TAIL = 8
PIECES = 4
F32 = jnp.float32
BF16 = jnp.bfloat16


def sign_table(size):
    a = lax.broadcasted_iota(jnp.int32, (size, size), 0)
    b = lax.broadcasted_iota(jnp.int32, (size, size), 1)
    x = jnp.bitwise_and(a, b)
    parity = jnp.zeros((size, size), jnp.int32)
    for bit in range(int(size).bit_length()):
        parity = jnp.bitwise_xor(parity, jnp.bitwise_and(jnp.right_shift(x, bit), 1))
    return (1 - 2 * parity).astype(F32)


def context_kernel(blocks, lens, q_ref, k_ref, v_ref, *refs, tq, tk, hp, st):
    pieces, o_ref, ak_ref, av_ref = refs[:PIECES], refs[-3], refs[-2], refs[-1]
    me = lax.axis_index("ctx")
    own_block = blocks[me]
    own_len = lens[own_block]
    anchor_len = jnp.where(own_block == 0, 0, lens[0])
    rows, hd = k_ref.shape
    piece = rows // PIECES

    @pl.when(pl.program_id(0) == 0)
    def _():
        for k in range(PIECES):
            at = pl.multiple_of(jnp.bitwise_xor(me % PIECES, k) * piece, piece)
            ak_ref[pl.ds(at, piece), :] = pieces[k][:piece]
            av_ref[pl.ds(at, piece), :] = pieces[k][piece:]

    c = hd**-0.5 * LOG2E

    def scores(na, h, i):
        q = [q_ref[i * tq : (i + 1) * tq, (h + e) * hd : (h + e + 1) * hd] for e in range(st)]
        q = jnp.concatenate(q, axis=0)
        parts = []
        if na:
            edge = (na - 1) * tk
            sa = lax.dot_general(q, ak_ref[: na * tk], NT, preferred_element_type=F32)
            col = lax.broadcasted_iota(jnp.int32, (1, tk), 1)
            if na > 1:
                parts.append((sa[:, :edge], av_ref, 0))
            parts.append((jnp.where(col < anchor_len - edge, sa[:, edge:], NEG), av_ref, edge))
        so = lax.dot_general(q, k_ref[: (i + 1) * tq], NT, preferred_element_type=F32)
        r0 = lax.broadcasted_iota(jnp.int32, (tq, tq), 0)
        c0 = lax.broadcasted_iota(jnp.int32, (tq, tq), 1)
        seen = c0 <= r0
        d = [jnp.where(seen, so[e * tq : (e + 1) * tq, i * tq :], NEG) for e in range(st)]
        if i:
            parts.append((so[:, : i * tq], v_ref, 0))
        parts.append((jnp.concatenate(d, axis=0), v_ref, i * tq))
        return parts

    def fold(op, xs):
        return functools.reduce(
            op, [x[:, a : a + 128] for x in xs for a in range(0, x.shape[1], 128)]
        )

    def finish(parts, h, i):
        m = jnp.max(fold(jnp.maximum, [p for p, _, _ in parts]), axis=1, keepdims=True)
        acc = 0.0
        powers = []
        for p, src, at in parts:
            e = jnp.exp2((p - m) * c)
            powers.append(e)
            acc = acc + jnp.dot(
                e.astype(BF16), src[at : at + p.shape[1]], preferred_element_type=F32
            )
        total = jnp.sum(fold(jnp.add, powers), axis=1, keepdims=True)
        row = lax.broadcasted_iota(jnp.int32, (tq, 1), 0) + i * tq
        for e in range(st):
            part = slice(e * tq, (e + 1) * tq)
            out = jnp.where(row < own_len, acc[part] / total[part], 0.0)
            o_ref[i * tq : (i + 1) * tq, (h + e) * hd : (h + e + 1) * hd] = out.astype(BF16)

    def body(na):
        pending = None
        for h in range(0, hp, st):
            for i in range(rows // tq):
                s = scores(na, h, i)
                if pending is not None:
                    finish(*pending)
                pending = (s, h, i)
        finish(*pending)

    top = rows // tk
    for na in range(1, top + 1):
        above = anchor_len > (na - 1) * tk if na > 1 else True
        below = anchor_len <= na * tk if na < top else True
        pl.when(jnp.logical_and(above, below))(functools.partial(body, na))


def context_attention(blocks, lens, q, k, v, anchors, first, count, into, tq=128, tk=512, hp=2, st=2):
    rows, width = q.shape
    hd = k.shape[1]
    heads = width // hd
    full = pl.BlockSpec((rows, hd), lambda h, *_: (0, 0))
    piece = pl.BlockSpec((2 * rows // PIECES, hd), lambda h, *_: (0, 0))
    wide = pl.BlockSpec((rows, hp * hd), lambda h, *_: (0, h + first // hp))
    more = [] if into is None else [into]
    return pl.pallas_call(
        functools.partial(context_kernel, tq=tq, tk=tk, hp=hp, st=st),
        grid_spec=pltpu.PrefetchScalarGridSpec(
            num_scalar_prefetch=2,
            grid=(count // hp,),
            in_specs=[wide, full, full] + [piece] * PIECES + [pl.BlockSpec(memory_space=pl.ANY)] * len(more),
            out_specs=wide,
            scratch_shapes=[pltpu.VMEM((rows, hd), BF16)] * 2,
        ),
        input_output_aliases={5 + PIECES: 0} if more else {},
        out_shape=jax.ShapeDtypeStruct(q.shape, q.dtype),
        compiler_params=pltpu.CompilerParams(vmem_limit_bytes=24 << 20),
        cost_estimate=pl.CostEstimate(
            flops=6 * count * rows * rows * hd,
            bytes_accessed=4 * rows * count * hd + 8 * rows * hd,
            transcendentals=count * rows * rows * 3 // 2,
        ),
        name="context_attention",
    )(blocks, lens, q, k, v, *anchors, *more)


def deal_kernel(k_ref, v_ref, q_ref, *outs):
    mine = lax.axis_index("ctx") % PIECES
    piece = k_ref.shape[0] // PIECES
    hd = k_ref.shape[1]
    q = q_ref[...].astype(F32)
    q = [q[:, a : a + hd] for a in range(0, q.shape[1], hd)]
    q = jnp.concatenate(q, axis=0).astype(BF16)
    for k in range(PIECES):
        at = pl.multiple_of(jnp.bitwise_xor(mine, k) * piece, piece)
        outs[k][:piece, :] = k_ref[pl.ds(at, piece), :]
        outs[k][piece : 2 * piece, :] = v_ref[pl.ds(at, piece), :]
        outs[k][2 * piece :, :] = q


def dealt(keys, values, queries):
    hd = keys.shape[1]
    whole = pl.BlockSpec(memory_space=pltpu.VMEM)
    rows = 2 * keys.shape[0] // PIECES + queries.size // hd
    return pl.pallas_call(
        deal_kernel,
        in_specs=[whole] * 3,
        out_specs=[whole] * PIECES,
        out_shape=[jax.ShapeDtypeStruct((rows, hd), keys.dtype)] * PIECES,
        compiler_params=pltpu.CompilerParams(vmem_limit_bytes=6 << 20),
        name="deal_pieces",
    )(keys, values, queries)


def differing(host_block):
    root = 0
    for i in range(host_block.shape[0]):
        root = root + jnp.where(host_block[i] == 0, i, 0)
    return jnp.bitwise_xor(root, lax.axis_index("ctx"))


def regroup_kernel(host_block, *refs, body):
    parts, o_ref = refs[:-1], refs[-1]
    differ = jnp.bitwise_and(differing(host_block), PIECES - 1)
    mine = lax.axis_index("ctx") % PIECES
    count = parts[0].shape[0] - body
    for k in range(PIECES):

        @pl.when(differ == k)
        def _():
            o_ref[:body, :] = parts[k][:body, :]

        at = pl.multiple_of(body + jnp.bitwise_xor(mine, k) * count, 16)
        o_ref[pl.ds(at, count), :] = parts[k][body:, :]


def regrouped(host_block, parts, body):
    whole = pl.BlockSpec(memory_space=pltpu.VMEM)
    rows, hd = parts[0].shape
    return pl.pallas_call(
        functools.partial(regroup_kernel, body=body),
        in_specs=[pl.BlockSpec(memory_space=pltpu.SMEM)] + [whole] * PIECES,
        out_specs=whole,
        out_shape=jax.ShapeDtypeStruct((body + PIECES * (rows - body), hd), parts[0].dtype),
        compiler_params=pltpu.CompilerParams(vmem_limit_bytes=4 << 20),
        name="regroup",
    )(host_block, *parts)


def far_kernel(host_block, own, got, *outs, body, bit, last):
    mine = jnp.bitwise_and(jnp.right_shift(lax.axis_index("ctx"), bit), 1)
    differ = jnp.bitwise_and(jnp.right_shift(differing(host_block), bit), 1)
    held, queries = outs if last else (outs[0].at[:body, :], outs[0].at[body:, :])
    count = own.shape[0] - body

    @pl.when(differ == 0)
    def _():
        held[...] = own[:body, :]

    @pl.when(differ == 1)
    def _():
        held[...] = got[:body, :]

    queries[pl.ds(pl.multiple_of(mine * count, 16), count), :] = own[body:, :]
    queries[pl.ds(pl.multiple_of((1 - mine) * count, 16), count), :] = got[body:, :]


def far_merged(host_block, own, got, body, bit, last):
    whole = pl.BlockSpec(memory_space=pltpu.VMEM)
    rows, hd = own.shape
    sizes = [body, 2 * (rows - body)]
    sizes = sizes if last else [sum(sizes)]
    return pl.pallas_call(
        functools.partial(far_kernel, body=body, bit=bit, last=last),
        in_specs=[pl.BlockSpec(memory_space=pltpu.SMEM)] + [whole] * 2,
        out_specs=[whole] * len(sizes),
        out_shape=[jax.ShapeDtypeStruct((r, hd), own.dtype) for r in sizes],
        compiler_params=pltpu.CompilerParams(vmem_limit_bytes=4 << 20),
        name="far_merge",
    )(host_block, own, got)


def store_kernel(k_ref, v_ref, key_ref, value_ref):
    hd = k_ref.shape[1]
    table = sign_table(hd).astype(BF16)

    def store(ref):
        r = jnp.dot(ref[...], table, preferred_element_type=F32) * hd**-0.5
        ceiling = CLIP_FACTOR * jnp.sqrt(jnp.mean(r * r, axis=-1, keepdims=True))
        return jnp.clip(r, -ceiling, ceiling)

    key_ref[...] = store(k_ref).astype(BF16)
    value_ref[...] = store(v_ref).T.astype(BF16)


def stored(keys, values):
    whole = pl.BlockSpec(memory_space=pltpu.VMEM)
    return pl.pallas_call(
        store_kernel,
        in_specs=[whole] * 2,
        out_specs=[whole] * 2,
        out_shape=[
            jax.ShapeDtypeStruct(keys.shape, BF16),
            jax.ShapeDtypeStruct(values.shape[::-1], BF16),
        ],
        compiler_params=pltpu.CompilerParams(vmem_limit_bytes=8 << 20),
        name="rotate_store",
    )(keys, values)


def partial_kernel(host_block, lens, q_ref, key_ref, value_ref, *refs, per, step):
    outs, turned = refs[:-1], refs[-1]
    me = lax.axis_index("ctx")
    spot = jnp.bitwise_and(jnp.right_shift(me, 1), SPREAD - 1)
    own_len = lens[host_block[me]]
    rows, hd = key_ref.shape
    scale = hd**-0.5
    hosts = host_block.shape[0]
    turned[...] = (
        jnp.dot(q_ref[...], sign_table(hd).astype(BF16), preferred_element_type=F32) * scale
    )
    usable = lax.broadcasted_iota(jnp.int32, (rows, 1), 0) < own_len
    for k in range(SPREAD):
        first = jnp.bitwise_xor(spot, k) * (per * step)
        rot = []
        for e in range(per):
            for c in range(hosts):
                at = pl.multiple_of(first + (c * SPREAD * per + e) * step, step)
                rot.append(turned[pl.ds(at, step), :])
        rot = jnp.concatenate(rot, axis=0).astype(BF16)
        s = lax.dot_general(key_ref[...], rot, NT, preferred_element_type=F32) * scale
        s = jnp.where(usable, s, NEG)
        m = jnp.max(s, axis=0, keepdims=True)
        p = jnp.exp(s - m)
        total = jnp.sum(p, axis=0, keepdims=True)
        outs[k][:hd, :] = jnp.dot(value_ref[...], p.astype(BF16), preferred_element_type=F32)
        outs[k][hd : hd + 1, :] = m
        outs[k][hd + 1 : hd + 2, :] = total
        outs[k][hd + 2 :, :] = jnp.zeros((TAIL - 2, rot.shape[0]), F32)


def host_partials(host_block, lens, queries, key_store, value_store, heads, step):
    hd = key_store.shape[1]
    rows = queries.shape[0]
    shape = jax.ShapeDtypeStruct((hd + TAIL, rows // SPREAD), F32)
    whole = pl.BlockSpec(memory_space=pltpu.VMEM)
    return pl.pallas_call(
        functools.partial(partial_kernel, per=heads // SPREAD, step=step),
        in_specs=[pl.BlockSpec(memory_space=pltpu.SMEM)] * 2 + [whole] * 3,
        out_specs=[whole] * SPREAD,
        out_shape=[shape] * SPREAD,
        scratch_shapes=[pltpu.VMEM((rows, hd), F32)],
        compiler_params=pltpu.CompilerParams(vmem_limit_bytes=16 << 20),
        name="host_partials",
    )(host_block, lens, queries, key_store, value_store)


def merge_values(parts, hd):
    maxima = [p[hd : hd + 1, :] for p in parts]
    overall = functools.reduce(jnp.maximum, maxima)
    factors = [jnp.exp(m - overall) for m in maxima]
    out = sum(p[:hd, :] * f for p, f in zip(parts, factors))
    total = sum(p[hd + 1 : hd + 2, :] * f for p, f in zip(parts, factors))
    return overall, total, out


def merge_kernel(*refs, hd):
    o_ref = refs[-1]
    overall, total, out = merge_values(refs[:-1], hd)
    o_ref[:hd, :] = out
    o_ref[hd : hd + 1, :] = overall
    o_ref[hd + 1 : hd + 2, :] = total
    o_ref[hd + 2 :, :] = jnp.zeros((TAIL - 2, out.shape[1]), F32)


def merged(parts, hd):
    whole = pl.BlockSpec(memory_space=pltpu.VMEM)
    return pl.pallas_call(
        functools.partial(merge_kernel, hd=hd),
        in_specs=[whole] * len(parts),
        out_specs=whole,
        out_shape=jax.ShapeDtypeStruct(parts[0].shape, F32),
        compiler_params=pltpu.CompilerParams(vmem_limit_bytes=4 << 20),
        name="merge_partials",
    )(*parts)


def finish_kernel(*refs, hd, tokens):
    o_ref = refs[-1]
    _, total, out = merge_values(refs[:-1], hd)
    turned = jnp.dot(
        sign_table(hd),
        out / total,
        preferred_element_type=F32,
        precision=lax.Precision.HIGHEST,
    )
    turned = (turned * hd**-0.5).T
    for e in range(turned.shape[0] // tokens):
        o_ref[:, e * hd : (e + 1) * hd] = turned[e * tokens : (e + 1) * tokens].astype(BF16)


def finished(parts, hd, tokens):
    whole = pl.BlockSpec(memory_space=pltpu.VMEM)
    per = parts[0].shape[1] // tokens
    return pl.pallas_call(
        functools.partial(finish_kernel, hd=hd, tokens=tokens),
        in_specs=[whole] * len(parts),
        out_specs=whole,
        out_shape=jax.ShapeDtypeStruct((tokens, per * hd), BF16),
        compiler_params=pltpu.CompilerParams(vmem_limit_bytes=4 << 20),
        name="finish_queries",
    )(*parts)


def project_kernel(*refs, groups):
    a_refs, w_ref, outs, total = refs[:SPREAD], refs[SPREAD], refs[SPREAD + 1 : -1], refs[-1]
    spot = jnp.bitwise_and(jnp.right_shift(lax.axis_index("ctx"), 1), SPREAD - 1)
    head = lax.axis_index("head")
    depth = a_refs[0].shape[1]
    acc = 0.0
    for k in range(SPREAD):
        at = pl.multiple_of(jnp.bitwise_xor(spot, k) * depth, depth)
        acc = acc + jnp.dot(a_refs[k][...], w_ref[pl.ds(at, depth), :], preferred_element_type=F32)
    total[...] = acc
    rows = total.shape[0] // groups
    for k in range(groups):
        at = pl.multiple_of(jnp.bitwise_xor(head, k) * rows, rows)
        outs[k][...] = total[pl.ds(at, rows), :]


def projected(chunks, weight, groups):
    tokens = chunks[0].shape[0]
    columns = weight.shape[1]
    whole = pl.BlockSpec(memory_space=pltpu.VMEM)
    return pl.pallas_call(
        functools.partial(project_kernel, groups=groups),
        in_specs=[whole] * (SPREAD + 1),
        out_specs=[whole] * groups,
        out_shape=[jax.ShapeDtypeStruct((tokens // groups, columns), F32)] * groups,
        scratch_shapes=[pltpu.VMEM((tokens, columns), F32)],
        compiler_params=pltpu.CompilerParams(vmem_limit_bytes=8 << 20),
        name="project",
    )(*chunks, weight)


def swap(x, axis, flip):
    size = lax.axis_size(axis)
    return lax.ppermute(x, axis, [(i, i ^ flip) for i in range(size)])


def per_device(
    ctx_queries, ctx_keys, ctx_values, new_queries, out_weight, host_block, block_lengths
):
    hosts = lax.axis_size("ctx")
    groups = lax.axis_size("head")
    bits = hosts.bit_length() - 1
    other_bits = [b for b in range(bits) if b not in SPREAD_BITS]
    heads = ctx_queries.shape[1] // HD
    tokens = new_queries.shape[0] * hosts
    body = 2 * ctx_keys.shape[0] // PIECES

    deal = list(dealt(ctx_keys, ctx_values, new_queries))
    keys, values, deal[0] = lax.optimization_barrier((ctx_keys, ctx_values, deal[0]))
    key_store, value_store = stored(keys, values)
    deal = [deal[0]] + [swap(deal[k], "ctx", k) for k in range(1, PIECES)]
    deal[0], key_store = lax.optimization_barrier((deal[0], key_store))
    message = regrouped(host_block, deal, body)
    for b in range(2, bits):
        message = far_merged(host_block, message, swap(message, "ctx", 1 << b), body, b, b == bits - 1)
        message = message if b == bits - 1 else message[0]
    held, all_queries = message
    anchors = [held] + [swap(held, "ctx", k) for k in range(1, PIECES)]

    partials = host_partials(
        host_block, block_lengths, all_queries, key_store, value_store, heads, new_queries.shape[0]
    )
    parts = [partials[0]] + [swap(partials[k], "ctx", k << 1) for k in range(1, SPREAD)]
    one = merged(parts, HD)
    for b in other_bits[1:]:
        one = merged([one, swap(one, "ctx", 1 << b)], HD)
    other = swap(one, "ctx", 1)

    def attend(anchors, first, count, into):
        return context_attention(
            host_block, block_lengths, ctx_queries, ctx_keys, ctx_values, anchors, first, count, into
        )

    counts = (heads // 4, heads // 2, heads // 4)
    anchors[0], one = lax.optimization_barrier((anchors[0], one))
    context_out = attend(anchors, 0, counts[0], None)
    one, context_out = lax.optimization_barrier((one, context_out))
    chunk = finished([one, other], HD, tokens)
    chunks = [chunk] + [swap(chunk, "ctx", k << 1) for k in range(1, SPREAD)]
    anchors[0], _ = lax.optimization_barrier((anchors[0], chunk))
    context_out = attend(anchors, counts[0], counts[1], context_out)
    chunks[0], context_out = lax.optimization_barrier((chunks[0], context_out))
    sums = projected(chunks, out_weight, groups)
    anchors[0], _ = lax.optimization_barrier((anchors[0], sums[0]))
    context_out = attend(anchors, counts[0] + counts[1], counts[2], context_out)
    answer = sums[0]
    for k in range(1, groups):
        answer = answer + swap(sums[k], "head", k)
    answer = answer.astype(BF16)
    return (context_out, answer)


def solution(mesh):
    placed = (
        P("ctx", "head"),
        P("ctx", "head"),
        P("ctx", "head"),
        P("ctx", "head"),
        P("head", "ctx"),
        P(),
        P(),
    )
    return jax.shard_map(
        per_device,
        mesh=mesh,
        in_specs=placed,
        out_specs=(P("ctx", "head"), P("head", "ctx")),
        check_vma=False,
    )
```

profile of v0, /device:TPU:0, one launch (start us, length us, event | category | flops | bytes accessed | tf_op | source)
XLA Modules:
  0.0 77.4 jit_solution(17532252852123565472)
XLA Ops:
  0.6 0.0 copy-start
  0.6 0.9 %copy-done = bf16[1024,128]{1,0:T(8,128)(2,1)S(1)} copy-done((bf16[1024,128]{1,0:T(8,128)(2,1)S(1)}, bf16[1024,128]{1,0:T(8,128)(2,1)}, u32[]{:S(2)}) %copy-start) | copy-done | bytes 262168
  1.6 0.9 %copy-done.3 = bf16[1024,128]{1,0:T(8,128)(2,1)S(1)} copy-done((bf16[1024,128]{1,0:T(8,128)(2,1)S(1)}, bf16[1024,128]{1,0:T(8,128)(2,1)}, u32[]{:S(2)}) %copy-start.3) | copy-done | bytes 262168
  2.5 0.7 copy-done.8
  3.3 3.0 %collective-permute-start = (bf16[576,128]{1,0:T(8,128)(2,1)S(1)}, bf16[576,128]{1,0:T(8,128)(2,1)S(1)}, u32[]{:S(2)}, u32[]{:S(2)}) collective-permute-start(bf16[576,128]{1,0:T(8,128)(2,1)S(1)} %get-tuple-element.37), channel_id=1, source_target_pairs={{0,4},{4,0},{8,12},{12,8},{16,20},{20,16},{24,28},{28,24},{1,5},{5... | collective-permute-start | bytes 442376 | tf_op jit(solution)/shard_map/ppermute | solution.py:401
  6.3 1.6 %collective-permute-start.1 = (bf16[576,128]{1,0:T(8,128)(2,1)S(1)}, bf16[576,128]{1,0:T(8,128)(2,1)S(1)}, u32[]{:S(2)}, u32[]{:S(2)}) collective-permute-start(bf16[576,128]{1,0:T(8,128)(2,1)S(1)} %get-tuple-element.38), channel_id=1, source_target_pairs={{0,8},{4,12},{8,0},{12,4},{16,24},{20,28},{24,16},{28,20},{1,9},{5... | collective-permute-start | bytes 442376 | tf_op jit(solution)/shard_map/ppermute | solution.py:401
  7.9 0.0 collective-permute-start.2
  7.9 0.9 %copy-done.1 = bf16[1024,128]{1,0:T(8,128)(2,1)S(1)} copy-done((bf16[1024,128]{1,0:T(8,128)(2,1)S(1)}, bf16[1024,128]{1,0:T(8,128)(2,1)}, u32[]{:S(2)}) %copy-start.1) | copy-done | bytes 262168
  8.9 0.9 %copy-done.4 = bf16[1024,128]{1,0:T(8,128)(2,1)S(1)} copy-done((bf16[1024,128]{1,0:T(8,128)(2,1)S(1)}, bf16[1024,128]{1,0:T(8,128)(2,1)}, u32[]{:S(2)}) %copy-start.4) | copy-done | bytes 262168
  9.8 1.0 %rotate_store.1 = (bf16[1024,128]{1,0:T(8,128)(2,1)S(1)}, bf16[128,1024]{1,0:T(8,128)(2,1)S(1)}) custom-call(bf16[1024,128]{1,0:T(8,128)(2,1)S(1)} %copy-done.1, bf16[1024,128]{1,0:T(8,128)(2,1)S(1)} %copy-done.4), custom_call_target="tpu_custom_call" | custom-call | tf_op jit(solution)/shard_map/rotate_store/pallas_call | solution.py:251
  10.8 0.0 collective-permute-done.refs_1_
  10.8 2.3 %collective-permute-done.1.refs_2_ = bf16[576,128]{1,0:T(8,128)(2,1)S(1)} collective-permute-done((bf16[576,128]{1,0:T(8,128)(2,1)S(1)}, bf16[576,128]{1,0:T(8,128)(2,1)S(1)}, u32[]{:S(2)}, u32[]{:S(2)}) %collective-permute-start.1) | collective-permute-done | bytes 147488 | tf_op jit(solution)/shard_map/ppermute | solution.py:401
  13.1 1.5 %collective-permute-done.2.refs_3_ = bf16[576,128]{1,0:T(8,128)(2,1)S(1)} collective-permute-done((bf16[576,128]{1,0:T(8,128)(2,1)S(1)}, bf16[576,128]{1,0:T(8,128)(2,1)S(1)}, u32[]{:S(2)}, u32[]{:S(2)}) %collective-permute-start.2) | collective-permute-done | bytes 147488 | tf_op jit(solution)/shard_map/ppermute | solution.py:401
  14.6 0.7 copy-done.9
  15.3 0.6 regroup.1.own
  15.9 2.8 %collective-permute-start.3 = (bf16[768,128]{1,0:T(8,128)(2,1)S(1)}, bf16[768,128]{1,0:T(8,128)(2,1)S(1)}, u32[]{:S(2)}, u32[]{:S(2)}) collective-permute-start(bf16[768,128]{1,0:T(8,128)(2,1)S(1)} %regroup.1.own), channel_id=1, source_target_pairs={{0,16},{4,20},{8,24},{12,28},{16,0},{20,4},{24,8},{28,12},{1,17},{... | collective-permute-start | bytes 589832 | tf_op jit(solution)/shard_map/ppermute | solution.py:401
  18.7 8.5 %collective-permute-done.3.got = bf16[768,128]{1,0:T(8,128)(2,1)S(1)} collective-permute-done((bf16[768,128]{1,0:T(8,128)(2,1)S(1)}, bf16[768,128]{1,0:T(8,128)(2,1)S(1)}, u32[]{:S(2)}, u32[]{:S(2)}) %collective-permute-start.3) | collective-permute-done | bytes 196640 | tf_op jit(solution)/shard_map/ppermute | solution.py:401
  27.1 0.6 far_merge.1
  27.7 2.3 %host_partials.1 = (f32[136,128]{1,0:T(8,128)S(1)}, f32[136,128]{1,0:T(8,128)S(1)}, f32[136,128]{1,0:T(8,128)S(1)}, f32[136,128]{1,0:T(8,128)S(1)}) custom-call(s32[8]{0:T(128)S(1)} %copy-done.9, s32[8]{0:T(128)S(1)} %copy-done.11, bf16[512,128]{1,0:T(8,128)(2,1)S(1)} %get-tuple-element.41.q_ref, bf16[1024,128]{1,0:T(8,128)(2,1)S(1)} %get-tuple-element.42.key_ref, ...), custom_call_target="tpu_custom_call" | custom-call | tf_op jit(solution)/shard_map/host_partials/pallas_call | solution.py:300
  30.0 0.4 collective-permute-start.4
  30.4 1.4 %collective-permute-start.7 = (bf16[512,128]{1,0:T(8,128)(2,1)S(1)}, bf16[512,128]{1,0:T(8,128)(2,1)S(1)}, u32[]{:S(2)}, u32[]{:S(2)}) collective-permute-start(bf16[512,128]{1,0:T(8,128)(2,1)S(1)} %get-tuple-element.55.refs_0_), channel_id=1, source_target_pairs={{0,4},{4,0},{8,12},{12,8},{16,20},{20,16},{24,28},{28,24},{1,5},{5... | collective-permute-start | bytes 393224 | tf_op jit(solution)/shard_map/ppermute | solution.py:401
  31.8 1.4 %collective-permute-start.8 = (bf16[512,128]{1,0:T(8,128)(2,1)S(1)}, bf16[512,128]{1,0:T(8,128)(2,1)S(1)}, u32[]{:S(2)}, u32[]{:S(2)}) collective-permute-start(bf16[512,128]{1,0:T(8,128)(2,1)S(1)} %get-tuple-element.55.refs_0_), channel_id=1, source_target_pairs={{0,8},{4,12},{8,0},{12,4},{16,24},{20,28},{24,16},{28,20},{1,9},{5... | collective-permute-start | bytes 393224 | tf_op jit(solution)/shard_map/ppermute | solution.py:401
  33.1 0.7 collective-permute-start.9
  33.9 3.4 %collective-permute-start.5 = (f32[136,128]{1,0:T(8,128)S(1)}, f32[136,128]{1,0:T(8,128)S(1)}, u32[]{:S(2)}, u32[]{:S(2)}) collective-permute-start(f32[136,128]{1,0:T(8,128)S(1)} %get-tuple-element.46), channel_id=1, source_target_pairs={{0,16},{4,20},{8,24},{12,28},{16,0},{20,4},{24,8},{28,12},{1,17},{... | collective-permute-start | bytes 208904 | tf_op jit(solution)/shard_map/ppermute | solution.py:401
  37.2 0.9 %collective-permute-start.6 = (f32[136,128]{1,0:T(8,128)S(1)}, f32[136,128]{1,0:T(8,128)S(1)}, u32[]{:S(2)}, u32[]{:S(2)}) collective-permute-start(f32[136,128]{1,0:T(8,128)S(1)} %get-tuple-element.47), channel_id=1, source_target_pairs={{0,24},{4,28},{8,16},{12,20},{16,8},{20,12},{24,0},{28,4},{1,25},{... | collective-permute-start | bytes 208904 | tf_op jit(solution)/shard_map/ppermute | solution.py:401
  38.1 1.9 %collective-permute-done.5.refs_2_ = f32[136,128]{1,0:T(8,128)S(1)} collective-permute-done((f32[136,128]{1,0:T(8,128)S(1)}, f32[136,128]{1,0:T(8,128)S(1)}, u32[]{:S(2)}, u32[]{:S(2)}) %collective-permute-start.5) | collective-permute-done | bytes 69664 | tf_op jit(solution)/shard_map/ppermute | solution.py:401
  40.0 5.1 %collective-permute-done.6.refs_3_ = f32[136,128]{1,0:T(8,128)S(1)} collective-permute-done((f32[136,128]{1,0:T(8,128)S(1)}, f32[136,128]{1,0:T(8,128)S(1)}, u32[]{:S(2)}, u32[]{:S(2)}) %collective-permute-start.6) | collective-permute-done | bytes 69664 | tf_op jit(solution)/shard_map/ppermute | solution.py:401
  45.2 0.0 copy-start.10
  45.2 0.4 collective-permute-start.10
  45.6 0.0 collective-permute-done.7.refs_1_
  45.6 0.0 collective-permute-done.8.refs_2_
  45.6 0.0 collective-permute-done.9.refs_3_
  45.6 6.4 %context_attention.3.refs_4_ = bf16[1024,1024]{1,0:T(8,128)(2,1)} custom-call(s32[8]{0:T(128)S(1)} %copy-done.9, s32[8]{0:T(128)S(1)} %copy-done.11, bf16[1024,1024]{1,0:T(8,128)(2,1)S(1)} %copy-done.7, bf16[1024,128]{1,0:T(8,128)(2,1)S(1)} %copy-done.2, bf16[1024,128]{1,0:T(8,128)(2,1)S(1)} %copy-done.5, bf16[512,128]{1,0:T(8,128)(2,1)S(1)} %get-tuple-element.55.refs_0_, ...), custom_call_target="tpu_custom_call" | custom-call | flops 1610612736 | bytes 2097152 | tf_op jit(solution)/shard_map/context_attention/pallas_call | solution.py:119
  52.0 0.0 collective-permute-done.10.refs_1_
  52.0 0.3 finish_queries.1.refs_0_
  52.4 0.0 copy-start.6
  52.4 0.1 collective-permute-start.11
  52.4 1.7 %collective-permute-start.12 = (bf16[64,256]{1,0:T(8,128)(2,1)S(1)}, bf16[64,256]{1,0:T(8,128)(2,1)S(1)}, u32[]{:S(2)}, u32[]{:S(2)}) collective-permute-start(bf16[64,256]{1,0:T(8,128)(2,1)S(1)} %finish_queries.1.refs_0_), channel_id=1, source_target_pairs={{0,16},{4,20},{8,24},{12,28},{16,0},{20,4},{24,8},{28,12},{1,17},{... | collective-permute-start | bytes 98312 | tf_op jit(solution)/shard_map/ppermute | solution.py:401
  54.2 2.6 %collective-permute-start.13 = (bf16[64,256]{1,0:T(8,128)(2,1)S(1)}, bf16[64,256]{1,0:T(8,128)(2,1)S(1)}, u32[]{:S(2)}, u32[]{:S(2)}) collective-permute-start(bf16[64,256]{1,0:T(8,128)(2,1)S(1)} %finish_queries.1.refs_0_), channel_id=1, source_target_pairs={{0,24},{4,28},{8,16},{12,20},{16,8},{20,12},{24,0},{28,4},{1,25},{... | collective-permute-start | bytes 98312 | tf_op jit(solution)/shard_map/ppermute | solution.py:401
  56.8 11.1 %context_attention.4.refs_4_ = bf16[1024,1024]{1,0:T(8,128)(2,1)} custom-call(s32[8]{0:T(128)S(1)} %copy-done.10, s32[8]{0:T(128)S(1)} %copy-done.11, bf16[1024,1024]{1,0:T(8,128)(2,1)S(1)} %copy-done.7, bf16[1024,128]{1,0:T(8,128)(2,1)S(1)} %copy-done.2, bf16[1024,128]{1,0:T(8,128)(2,1)S(1)} %copy-done.5, ...), custom_call_target="tpu_custom_call", output_to_operand_aliasing={{}: (9, {})} | custom-call | flops 3221225472 | bytes 3145728 | tf_op jit(solution)/shard_map/context_attention/pallas_call | solution.py:119
  67.9 0.5 project.1
  68.5 0.1 collective-permute-start.14
  68.5 1.6 %collective-permute-start.15 = (f32[16,1024]{1,0:T(8,128)S(1)}, f32[16,1024]{1,0:T(8,128)S(1)}, u32[]{:S(2)}, u32[]{:S(2)}) collective-permute-start(f32[16,1024]{1,0:T(8,128)S(1)} %get-tuple-element.58), channel_id=1, source_target_pairs={{0,2},{1,3},{2,0},{3,1},{4,6},{5,7},{6,4},{7,5},{8,10},{9,11},{10,... | collective-permute-start | bytes 196616 | tf_op jit(solution)/shard_map/ppermute | solution.py:401
  70.1 0.3 collective-permute-start.16
  70.4 6.4 %context_attention.5 = bf16[1024,1024]{1,0:T(8,128)(2,1)} custom-call(s32[8]{0:T(128)S(1)} %copy-done.10, s32[8]{0:T(128)S(1)} %copy-done.11, bf16[1024,1024]{1,0:T(8,128)(2,1)S(1)} %copy-done.7, bf16[1024,128]{1,0:T(8,128)(2,1)S(1)} %copy-done.2, bf16[1024,128]{1,0:T(8,128)(2,1)S(1)} %copy-done.5, ...), custom_call_target="tpu_custom_call", output_to_operand_aliasing={{}: (9, {})} | custom-call | flops 1610612736 | bytes 2097152 | tf_op jit(solution)/shard_map/context_attention/pallas_call | solution.py:119
  76.8 0.0 collective-permute-done.14
  76.8 0.0 collective-permute-done.15
  76.8 0.6 add_convert_fusion
  (22 shorter events, 0.1 us)
Async XLA Ops:
  0.6 1.0 %copy-start = (bf16[1024,128]{1,0:T(8,128)(2,1)S(1)}, bf16[1024,128]{1,0:T(8,128)(2,1)}, u32[]{:S(2)}) copy-start(bf16[1024,128]{1,0:T(8,128)(2,1)} %k_ref.8) | copy-start | bytes 786436
  1.6 0.9 %copy-start.3 = (bf16[1024,128]{1,0:T(8,128)(2,1)S(1)}, bf16[1024,128]{1,0:T(8,128)(2,1)}, u32[]{:S(2)}) copy-start(bf16[1024,128]{1,0:T(8,128)(2,1)} %v_ref.8) | copy-start | bytes 786436
  2.5 0.7 copy-start.8
  3.3 24.5 %copy-start.11 = (s32[8]{0:T(128)S(1)}, s32[8]{0:T(128)}, u32[]{:S(2)}) copy-start(s32[8]{0:T(128)} %lens.7) | copy-start | bytes 100
  3.3 42.4 %copy-start.2 = (bf16[1024,128]{1,0:T(8,128)(2,1)S(1)}, bf16[1024,128]{1,0:T(8,128)(2,1)}, u32[]{:S(2)}) copy-start(bf16[1024,128]{1,0:T(8,128)(2,1)} %k_ref.8) | copy-start | bytes 786436
  3.3 42.4 %copy-start.5 = (bf16[1024,128]{1,0:T(8,128)(2,1)S(1)}, bf16[1024,128]{1,0:T(8,128)(2,1)}, u32[]{:S(2)}) copy-start(bf16[1024,128]{1,0:T(8,128)(2,1)} %v_ref.8) | copy-start | bytes 786436
  3.3 7.5 %collective-permute-start = (bf16[576,128]{1,0:T(8,128)(2,1)S(1)}, bf16[576,128]{1,0:T(8,128)(2,1)S(1)}, u32[]{:S(2)}, u32[]{:S(2)}) collective-permute-start(bf16[576,128]{1,0:T(8,128)(2,1)S(1)} %get-tuple-element.37), channel_id=1, source_target_pairs={{0,4},{4,0},{8,12},{12,8},{16,20},{20,16},{24,28},{28,24},{1,5},{5... | collective-permute-start | bytes 442376 | tf_op jit(solution)/shard_map/ppermute | solution.py:401
  6.3 6.8 %collective-permute-start.1 = (bf16[576,128]{1,0:T(8,128)(2,1)S(1)}, bf16[576,128]{1,0:T(8,128)(2,1)S(1)}, u32[]{:S(2)}, u32[]{:S(2)}) collective-permute-start(bf16[576,128]{1,0:T(8,128)(2,1)S(1)} %get-tuple-element.38), channel_id=1, source_target_pairs={{0,8},{4,12},{8,0},{12,4},{16,24},{20,28},{24,16},{28,20},{1,9},{5... | collective-permute-start | bytes 442376 | tf_op jit(solution)/shard_map/ppermute | solution.py:401
  7.9 6.7 %collective-permute-start.2 = (bf16[576,128]{1,0:T(8,128)(2,1)S(1)}, bf16[576,128]{1,0:T(8,128)(2,1)S(1)}, u32[]{:S(2)}, u32[]{:S(2)}) collective-permute-start(bf16[576,128]{1,0:T(8,128)(2,1)S(1)} %get-tuple-element.39), channel_id=1, source_target_pairs={{0,12},{4,8},{8,4},{12,0},{16,28},{20,24},{24,20},{28,16},{1,13},{... | collective-permute-start | bytes 442376 | tf_op jit(solution)/shard_map/ppermute | solution.py:401
  7.9 1.0 %copy-start.1 = (bf16[1024,128]{1,0:T(8,128)(2,1)S(1)}, bf16[1024,128]{1,0:T(8,128)(2,1)}, u32[]{:S(2)}) copy-start(bf16[1024,128]{1,0:T(8,128)(2,1)} %k_ref.8) | copy-start | bytes 786436
  8.9 0.9 %copy-start.4 = (bf16[1024,128]{1,0:T(8,128)(2,1)S(1)}, bf16[1024,128]{1,0:T(8,128)(2,1)}, u32[]{:S(2)}) copy-start(bf16[1024,128]{1,0:T(8,128)(2,1)} %v_ref.8) | copy-start | bytes 786436
  9.8 35.8 %copy-start.7 = (bf16[1024,1024]{1,0:T(8,128)(2,1)S(1)}, bf16[1024,1024]{1,0:T(8,128)(2,1)}, u32[]{:S(2)}) copy-start(bf16[1024,1024]{1,0:T(8,128)(2,1)} %q_ref.7) | copy-start | bytes 6291460
  14.6 0.7 copy-start.9
  15.9 11.3 %collective-permute-start.3 = (bf16[768,128]{1,0:T(8,128)(2,1)S(1)}, bf16[768,128]{1,0:T(8,128)(2,1)S(1)}, u32[]{:S(2)}, u32[]{:S(2)}) collective-permute-start(bf16[768,128]{1,0:T(8,128)(2,1)S(1)} %regroup.1.own), channel_id=1, source_target_pairs={{0,16},{4,20},{8,24},{12,28},{16,0},{20,4},{24,8},{28,12},{1,17},{... | collective-permute-start | bytes 589832 | tf_op jit(solution)/shard_map/ppermute | solution.py:401
  30.0 7.2 %collective-permute-start.4 = (f32[136,128]{1,0:T(8,128)S(1)}, f32[136,128]{1,0:T(8,128)S(1)}, u32[]{:S(2)}, u32[]{:S(2)}) collective-permute-start(f32[136,128]{1,0:T(8,128)S(1)} %get-tuple-element.45), channel_id=1, source_target_pairs={{0,8},{4,12},{8,0},{12,4},{16,24},{20,28},{24,16},{28,20},{1,9},{5... | collective-permute-start | bytes 208904 | tf_op jit(solution)/shard_map/ppermute | solution.py:401
  30.4 15.2 %collective-permute-start.7 = (bf16[512,128]{1,0:T(8,128)(2,1)S(1)}, bf16[512,128]{1,0:T(8,128)(2,1)S(1)}, u32[]{:S(2)}, u32[]{:S(2)}) collective-permute-start(bf16[512,128]{1,0:T(8,128)(2,1)S(1)} %get-tuple-element.55.refs_0_), channel_id=1, source_target_pairs={{0,4},{4,0},{8,12},{12,8},{16,20},{20,16},{24,28},{28,24},{1,5},{5... | collective-permute-start | bytes 393224 | tf_op jit(solution)/shard_map/ppermute | solution.py:401
  31.8 13.8 %collective-permute-start.8 = (bf16[512,128]{1,0:T(8,128)(2,1)S(1)}, bf16[512,128]{1,0:T(8,128)(2,1)S(1)}, u32[]{:S(2)}, u32[]{:S(2)}) collective-permute-start(bf16[512,128]{1,0:T(8,128)(2,1)S(1)} %get-tuple-element.55.refs_0_), channel_id=1, source_target_pairs={{0,8},{4,12},{8,0},{12,4},{16,24},{20,28},{24,16},{28,20},{1,9},{5... | collective-permute-start | bytes 393224 | tf_op jit(solution)/shard_map/ppermute | solution.py:401
  33.1 12.5 %collective-permute-start.9 = (bf16[512,128]{1,0:T(8,128)(2,1)S(1)}, bf16[512,128]{1,0:T(8,128)(2,1)S(1)}, u32[]{:S(2)}, u32[]{:S(2)}) collective-permute-start(bf16[512,128]{1,0:T(8,128)(2,1)S(1)} %get-tuple-element.55.refs_0_), channel_id=1, source_target_pairs={{0,12},{4,8},{8,4},{12,0},{16,28},{20,24},{24,20},{28,16},{1,13},{... | collective-permute-start | bytes 393224 | tf_op jit(solution)/shard_map/ppermute | solution.py:401
  33.9 6.2 %collective-permute-start.5 = (f32[136,128]{1,0:T(8,128)S(1)}, f32[136,128]{1,0:T(8,128)S(1)}, u32[]{:S(2)}, u32[]{:S(2)}) collective-permute-start(f32[136,128]{1,0:T(8,128)S(1)} %get-tuple-element.46), channel_id=1, source_target_pairs={{0,16},{4,20},{8,24},{12,28},{16,0},{20,4},{24,8},{28,12},{1,17},{... | collective-permute-start | bytes 208904 | tf_op jit(solution)/shard_map/ppermute | solution.py:401
  37.2 7.9 %collective-permute-start.6 = (f32[136,128]{1,0:T(8,128)S(1)}, f32[136,128]{1,0:T(8,128)S(1)}, u32[]{:S(2)}, u32[]{:S(2)}) collective-permute-start(f32[136,128]{1,0:T(8,128)S(1)} %get-tuple-element.47), channel_id=1, source_target_pairs={{0,24},{4,28},{8,16},{12,20},{16,8},{20,12},{24,0},{28,4},{1,25},{... | collective-permute-start | bytes 208904 | tf_op jit(solution)/shard_map/ppermute | solution.py:401
  45.2 11.7 %copy-start.10 = (s32[8]{0:T(128)S(1)}, s32[8]{0:T(128)}, u32[]{:S(2)}) copy-start(s32[8]{0:T(128)} %blocks.5) | copy-start | bytes 100
  45.2 6.8 %collective-permute-start.10 = (f32[136,128]{1,0:T(8,128)S(1)}, f32[136,128]{1,0:T(8,128)S(1)}, u32[]{:S(2)}, u32[]{:S(2)}) collective-permute-start(f32[136,128]{1,0:T(8,128)S(1)} %merge_partials.1.refs_0_), channel_id=1, source_target_pairs={{0,4},{4,0},{8,12},{12,8},{16,20},{20,16},{24,28},{28,24},{1,5},{5... | collective-permute-start | bytes 208904 | tf_op jit(solution)/shard_map/ppermute | solution.py:401
  52.4 15.6 %copy-start.6 = (bf16[1024,1024]{1,0:T(8,128)(2,1)S(1)}, bf16[1024,1024]{1,0:T(8,128)(2,1)}, u32[]{:S(2)}) copy-start(bf16[1024,1024]{1,0:T(8,128)(2,1)} %refs_4_.1) | copy-start | bytes 6291460
  52.4 15.5 %collective-permute-start.11 = (bf16[64,256]{1,0:T(8,128)(2,1)S(1)}, bf16[64,256]{1,0:T(8,128)(2,1)S(1)}, u32[]{:S(2)}, u32[]{:S(2)}) collective-permute-start(bf16[64,256]{1,0:T(8,128)(2,1)S(1)} %finish_queries.1.refs_0_), channel_id=1, source_target_pairs={{0,8},{4,12},{8,0},{12,4},{16,24},{20,28},{24,16},{28,20},{1,9},{5... | collective-permute-start | bytes 98312 | tf_op jit(solution)/shard_map/ppermute | solution.py:401
  52.4 15.5 %collective-permute-start.12 = (bf16[64,256]{1,0:T(8,128)(2,1)S(1)}, bf16[64,256]{1,0:T(8,128)(2,1)S(1)}, u32[]{:S(2)}, u32[]{:S(2)}) collective-permute-start(bf16[64,256]{1,0:T(8,128)(2,1)S(1)} %finish_queries.1.refs_0_), channel_id=1, source_target_pairs={{0,16},{4,20},{8,24},{12,28},{16,0},{20,4},{24,8},{28,12},{1,17},{... | collective-permute-start | bytes 98312 | tf_op jit(solution)/shard_map/ppermute | solution.py:401
  54.2 13.7 %collective-permute-start.13 = (bf16[64,256]{1,0:T(8,128)(2,1)S(1)}, bf16[64,256]{1,0:T(8,128)(2,1)S(1)}, u32[]{:S(2)}, u32[]{:S(2)}) collective-permute-start(bf16[64,256]{1,0:T(8,128)(2,1)S(1)} %finish_queries.1.refs_0_), channel_id=1, source_target_pairs={{0,24},{4,28},{8,16},{12,20},{16,8},{20,12},{24,0},{28,4},{1,25},{... | collective-permute-start | bytes 98312 | tf_op jit(solution)/shard_map/ppermute | solution.py:401
  68.5 8.3 %collective-permute-start.14 = (f32[16,1024]{1,0:T(8,128)S(1)}, f32[16,1024]{1,0:T(8,128)S(1)}, u32[]{:S(2)}, u32[]{:S(2)}) collective-permute-start(f32[16,1024]{1,0:T(8,128)S(1)} %get-tuple-element.57), channel_id=1, source_target_pairs={{0,1},{1,0},{2,3},{3,2},{4,5},{5,4},{6,7},{7,6},{8,9},{9,8},{10,11... | collective-permute-start | bytes 196616 | tf_op jit(solution)/shard_map/ppermute | solution.py:401
  68.5 8.3 %collective-permute-start.15 = (f32[16,1024]{1,0:T(8,128)S(1)}, f32[16,1024]{1,0:T(8,128)S(1)}, u32[]{:S(2)}, u32[]{:S(2)}) collective-permute-start(f32[16,1024]{1,0:T(8,128)S(1)} %get-tuple-element.58), channel_id=1, source_target_pairs={{0,2},{1,3},{2,0},{3,1},{4,6},{5,7},{6,4},{7,5},{8,10},{9,11},{10,... | collective-permute-start | bytes 196616 | tf_op jit(solution)/shard_map/ppermute | solution.py:401
  70.1 6.7 %collective-permute-start.16 = (f32[16,1024]{1,0:T(8,128)S(1)}, f32[16,1024]{1,0:T(8,128)S(1)}, u32[]{:S(2)}, u32[]{:S(2)}) collective-permute-start(f32[16,1024]{1,0:T(8,128)S(1)} %get-tuple-element.59), channel_id=1, source_target_pairs={{0,3},{1,2},{2,1},{3,0},{4,7},{5,6},{6,5},{7,4},{8,11},{9,10},{10,... | collective-permute-start | bytes 196616 | tf_op jit(solution)/shard_map/ppermute | solution.py:401
where the time goes:
time: 77.7 us; the launch traced here: 77.4 us
  Pallas kernels  29.2 us (38%)
  starting transfers between devices  22.3 us (29%)
  waiting for transfers between devices  19.3 us (25%)
  local copies, waits for them, and re-layouts  5.19 us (7%)
  between operations  0.81 us (1%)
    pallas_call x3, Pallas kernels, context_attention(): pl.pallas_call(functools.partial(context_kernel, tq=tq, tk=tk, hp=hp, st=...  23.8 us
    ppermute x17, starting transfers between devices, swap(): return lax.ppermute(x, axis, [(i, i ^ flip) for i in range(size)])  22.3 us
    ppermute x17, waiting for transfers between devices, swap(): return lax.ppermute(x, axis, [(i, i ^ flip) for i in range(size)])  19.3 us
    unnamed x24, local copies, waits for them, and re-layouts  5.19 us
    pallas_call x1, Pallas kernels, host_partials(): pl.pallas_call(functools.partial(partial_kernel, per=heads // SPREAD, ste...  2.27 us
  transfers between devices with their start and end apart: 17, of which 5 were waited for; matrix products, arithmetic and copies ran while one was open for 0% of the time, Pallas kernels for 32%

commit v1 on v0

--- a/solution.py
+++ b/solution.py
@@ -108,7 +108,7 @@
         pl.when(jnp.logical_and(above, below))(functools.partial(body, na))
 
 
-def context_attention(blocks, lens, q, k, v, anchors, first, count, into, tq=128, tk=512, hp=2, st=2):
+def context_attention(blocks, lens, q, k, v, anchors, first, count, into, tq=128, tk=256, hp=2, st=2):
     rows, width = q.shape
     hd = k.shape[1]
     heads = width // hd
@@ -438,18 +438,15 @@
             host_block, block_lengths, ctx_queries, ctx_keys, ctx_values, anchors, first, count, into
         )
 
-    counts = (heads // 4, heads // 2, heads // 4)
-    anchors[0], one = lax.optimization_barrier((anchors[0], one))
-    context_out = attend(anchors, 0, counts[0], None)
-    one, context_out = lax.optimization_barrier((one, context_out))
+    half = heads // 2
     chunk = finished([one, other], HD, tokens)
     chunks = [chunk] + [swap(chunk, "ctx", k << 1) for k in range(1, SPREAD)]
     anchors[0], _ = lax.optimization_barrier((anchors[0], chunk))
-    context_out = attend(anchors, counts[0], counts[1], context_out)
+    context_out = attend(anchors, 0, half, None)
     chunks[0], context_out = lax.optimization_barrier((chunks[0], context_out))
     sums = projected(chunks, out_weight, groups)
     anchors[0], _ = lax.optimization_barrier((anchors[0], sums[0]))
-    context_out = attend(anchors, counts[0] + counts[1], counts[2], context_out)
+    context_out = attend(anchors, half, half, context_out)
     answer = sums[0]
     for k in range(1, groups):
         answer = answer + swap(sums[k], "head", k)

time: 77.7 us -> 75.4 us (0.970)
  waiting for transfers between devices: 19.3 us -> 17.2 us
  Pallas kernels: 29.2 us -> 27.7 us
  starting transfers between devices: 22.3 us -> 23.5 us
    ppermute x17, waiting for transfers between devices: 19.3 us -> 17.2 us  [swap(): return lax.ppermute(x, axis, [(i, i ^ flip) for i in range(size)])]
    pallas_call x3 -> x2, Pallas kernels: 23.8 us -> 22.4 us  [context_attention(): pl.pallas_call(functools.partial(context_kernel, tq=tq, tk=tk, hp=hp, st=...]
    ppermute x17, starting transfers between devices: 22.3 us -> 23.5 us  [swap(): return lax.ppermute(x, axis, [(i, i ^ flip) for i in range(size)])]
  transfers between devices with their start and end apart: 17 -> 17, of which waited for: 5 -> 6; matrix products, arithmetic and copies ran while one was open for 0% -> 0% of each run, Pallas kernels for 32% -> 32%
where the time goes in v1:
time: 75.4 us; the launch traced here: 75.1 us
  Pallas kernels  27.7 us (37%)
  starting transfers between devices  23.5 us (31%)
  waiting for transfers between devices  17.2 us (23%)
  local copies, waits for them, and re-layouts  5.19 us (7%)
  between operations  0.8 us (1%)
    ppermute x17, starting transfers between devices, swap(): return lax.ppermute(x, axis, [(i, i ^ flip) for i in range(size)])  23.5 us
    pallas_call x2, Pallas kernels, context_attention(): pl.pallas_call(functools.partial(context_kernel, tq=tq, tk=tk, hp=hp, st=...  22.4 us
    ppermute x17, waiting for transfers between devices, swap(): return lax.ppermute(x, axis, [(i, i ^ flip) for i in range(size)])  17.2 us
    unnamed x24, local copies, waits for them, and re-layouts  5.19 us
    pallas_call x1, Pallas kernels, host_partials(): pl.pallas_call(functools.partial(partial_kernel, per=heads // SPREAD, ste...  2.27 us
  transfers between devices with their start and end apart: 17, of which 6 were waited for; matrix products, arithmetic and copies ran while one was open for 0% of the time, Pallas kernels for 32%

profile of v1, /device:TPU:0, one launch (start us, length us, event | category | flops | bytes accessed | tf_op | source)
XLA Modules:
  0.0 75.1 jit_solution(17997550812320845494)
XLA Ops:
  0.6 0.0 copy-start.1
  0.6 0.9 %copy-done.1 = bf16[1024,128]{1,0:T(8,128)(2,1)S(1)} copy-done((bf16[1024,128]{1,0:T(8,128)(2,1)S(1)}, bf16[1024,128]{1,0:T(8,128)(2,1)}, u32[]{:S(2)}) %copy-start.1) | copy-done | bytes 262168
  1.6 0.9 %copy-done.4 = bf16[1024,128]{1,0:T(8,128)(2,1)S(1)} copy-done((bf16[1024,128]{1,0:T(8,128)(2,1)S(1)}, bf16[1024,128]{1,0:T(8,128)(2,1)}, u32[]{:S(2)}) %copy-start.4) | copy-done | bytes 262168
  2.5 0.7 copy-done.7
  3.3 0.1 deal_pieces.1
  3.3 3.0 %collective-permute-start = (bf16[576,128]{1,0:T(8,128)(2,1)S(1)}, bf16[576,128]{1,0:T(8,128)(2,1)S(1)}, u32[]{:S(2)}, u32[]{:S(2)}) collective-permute-start(bf16[576,128]{1,0:T(8,128)(2,1)S(1)} %get-tuple-element.33), channel_id=1, source_target_pairs={{0,4},{4,0},{8,12},{12,8},{16,20},{20,16},{24,28},{28,24},{1,5},{5... | collective-permute-start | bytes 442376 | tf_op jit(solution)/shard_map/ppermute | solution.py:401
  6.4 1.6 %collective-permute-start.1 = (bf16[576,128]{1,0:T(8,128)(2,1)S(1)}, bf16[576,128]{1,0:T(8,128)(2,1)S(1)}, u32[]{:S(2)}, u32[]{:S(2)}) collective-permute-start(bf16[576,128]{1,0:T(8,128)(2,1)S(1)} %get-tuple-element.34), channel_id=1, source_target_pairs={{0,8},{4,12},{8,0},{12,4},{16,24},{20,28},{24,16},{28,20},{1,9},{5... | collective-permute-start | bytes 442376 | tf_op jit(solution)/shard_map/ppermute | solution.py:401
  7.9 0.0 collective-permute-start.2
  7.9 0.9 %copy-done.2 = bf16[1024,128]{1,0:T(8,128)(2,1)S(1)} copy-done((bf16[1024,128]{1,0:T(8,128)(2,1)S(1)}, bf16[1024,128]{1,0:T(8,128)(2,1)}, u32[]{:S(2)}) %copy-start.2) | copy-done | bytes 262168
  8.9 0.9 %copy-done.5 = bf16[1024,128]{1,0:T(8,128)(2,1)S(1)} copy-done((bf16[1024,128]{1,0:T(8,128)(2,1)S(1)}, bf16[1024,128]{1,0:T(8,128)(2,1)}, u32[]{:S(2)}) %copy-start.5) | copy-done | bytes 262168
  9.8 1.0 %rotate_store.1 = (bf16[1024,128]{1,0:T(8,128)(2,1)S(1)}, bf16[128,1024]{1,0:T(8,128)(2,1)S(1)}) custom-call(bf16[1024,128]{1,0:T(8,128)(2,1)S(1)} %copy-done.2, bf16[1024,128]{1,0:T(8,128)(2,1)S(1)} %copy-done.5), custom_call_target="tpu_custom_call" | custom-call | tf_op jit(solution)/shard_map/rotate_store/pallas_call | solution.py:251
  10.8 0.0 collective-permute-done.refs_1_
  10.8 2.3 %collective-permute-done.1.refs_2_ = bf16[576,128]{1,0:T(8,128)(2,1)S(1)} collective-permute-done((bf16[576,128]{1,0:T(8,128)(2,1)S(1)}, bf16[576,128]{1,0:T(8,128)(2,1)S(1)}, u32[]{:S(2)}, u32[]{:S(2)}) %collective-permute-start.1) | collective-permute-done | bytes 147488 | tf_op jit(solution)/shard_map/ppermute | solution.py:401
  13.1 1.5 %collective-permute-done.2.refs_3_ = bf16[576,128]{1,0:T(8,128)(2,1)S(1)} collective-permute-done((bf16[576,128]{1,0:T(8,128)(2,1)S(1)}, bf16[576,128]{1,0:T(8,128)(2,1)S(1)}, u32[]{:S(2)}, u32[]{:S(2)}) %collective-permute-start.2) | collective-permute-done | bytes 147488 | tf_op jit(solution)/shard_map/ppermute | solution.py:401
  14.6 0.7 copy-done.8
  15.3 0.6 regroup.1.own
  15.9 2.8 %collective-permute-start.3 = (bf16[768,128]{1,0:T(8,128)(2,1)S(1)}, bf16[768,128]{1,0:T(8,128)(2,1)S(1)}, u32[]{:S(2)}, u32[]{:S(2)}) collective-permute-start(bf16[768,128]{1,0:T(8,128)(2,1)S(1)} %regroup.1.own), channel_id=1, source_target_pairs={{0,16},{4,20},{8,24},{12,28},{16,0},{20,4},{24,8},{28,12},{1,17},{... | collective-permute-start | bytes 589832 | tf_op jit(solution)/shard_map/ppermute | solution.py:401
  18.7 8.5 %collective-permute-done.3.got = bf16[768,128]{1,0:T(8,128)(2,1)S(1)} collective-permute-done((bf16[768,128]{1,0:T(8,128)(2,1)S(1)}, bf16[768,128]{1,0:T(8,128)(2,1)S(1)}, u32[]{:S(2)}, u32[]{:S(2)}) %collective-permute-start.3) | collective-permute-done | bytes 196640 | tf_op jit(solution)/shard_map/ppermute | solution.py:401
  27.1 0.6 far_merge.1
  27.7 2.3 %host_partials.1 = (f32[136,128]{1,0:T(8,128)S(1)}, f32[136,128]{1,0:T(8,128)S(1)}, f32[136,128]{1,0:T(8,128)S(1)}, f32[136,128]{1,0:T(8,128)S(1)}) custom-call(s32[8]{0:T(128)S(1)} %copy-done.8, s32[8]{0:T(128)S(1)} %copy-done.10, bf16[512,128]{1,0:T(8,128)(2,1)S(1)} %get-tuple-element.37.q_ref, bf16[1024,128]{1,0:T(8,128)(2,1)S(1)} %get-tuple-element.38.key_ref, ...), custom_call_target="tpu_custom_call" | custom-call | tf_op jit(solution)/shard_map/host_partials/pallas_call | solution.py:300
  30.0 0.4 collective-permute-start.4
  30.4 3.4 %collective-permute-start.5 = (f32[136,128]{1,0:T(8,128)S(1)}, f32[136,128]{1,0:T(8,128)S(1)}, u32[]{:S(2)}, u32[]{:S(2)}) collective-permute-start(f32[136,128]{1,0:T(8,128)S(1)} %get-tuple-element.42), channel_id=1, source_target_pairs={{0,16},{4,20},{8,24},{12,28},{16,0},{20,4},{24,8},{28,12},{1,17},{... | collective-permute-start | bytes 208904 | tf_op jit(solution)/shard_map/ppermute | solution.py:401
  33.8 0.7 collective-permute-start.6
  34.5 0.7 collective-permute-start.10
  35.2 0.6 collective-permute-start.8
  35.8 0.0 collective-permute-done.4.refs_1_
  35.8 2.2 %collective-permute-start.9 = (bf16[512,128]{1,0:T(8,128)(2,1)S(1)}, bf16[512,128]{1,0:T(8,128)(2,1)S(1)}, u32[]{:S(2)}, u32[]{:S(2)}) collective-permute-start(bf16[512,128]{1,0:T(8,128)(2,1)S(1)} %get-tuple-element.47.refs_0_), channel_id=1, source_target_pairs={{0,8},{4,12},{8,0},{12,4},{16,24},{20,28},{24,16},{28,20},{1,9},{5... | collective-permute-start | bytes 393224 | tf_op jit(solution)/shard_map/ppermute | solution.py:401
  38.0 0.4 collective-permute-done.5.refs_2_
  38.3 1.9 %collective-permute-done.6.refs_3_ = f32[136,128]{1,0:T(8,128)S(1)} collective-permute-done((f32[136,128]{1,0:T(8,128)S(1)}, f32[136,128]{1,0:T(8,128)S(1)}, u32[]{:S(2)}, u32[]{:S(2)}) %collective-permute-start.6) | collective-permute-done | bytes 69664 | tf_op jit(solution)/shard_map/ppermute | solution.py:401
  40.3 1.8 %collective-permute-start.7 = (f32[136,128]{1,0:T(8,128)S(1)}, f32[136,128]{1,0:T(8,128)S(1)}, u32[]{:S(2)}, u32[]{:S(2)}) collective-permute-start(f32[136,128]{1,0:T(8,128)S(1)} %merge_partials.1.refs_0_), channel_id=1, source_target_pairs={{0,4},{4,0},{8,12},{12,8},{16,20},{20,16},{24,28},{28,24},{1,5},{5... | collective-permute-start | bytes 208904 | tf_op jit(solution)/shard_map/ppermute | solution.py:401
  42.1 2.6 %collective-permute-done.7.refs_1_ = f32[136,128]{1,0:T(8,128)S(1)} collective-permute-done((f32[136,128]{1,0:T(8,128)S(1)}, f32[136,128]{1,0:T(8,128)S(1)}, u32[]{:S(2)}, u32[]{:S(2)}) %collective-permute-start.7) | collective-permute-done | bytes 69664 | tf_op jit(solution)/shard_map/ppermute | solution.py:401
  44.7 0.3 finish_queries.1.refs_0_
  45.1 0.0 copy-start
  45.1 0.8 %collective-permute-start.11 = (bf16[64,256]{1,0:T(8,128)(2,1)S(1)}, bf16[64,256]{1,0:T(8,128)(2,1)S(1)}, u32[]{:S(2)}, u32[]{:S(2)}) collective-permute-start(bf16[64,256]{1,0:T(8,128)(2,1)S(1)} %finish_queries.1.refs_0_), channel_id=1, source_target_pairs={{0,8},{4,12},{8,0},{12,4},{16,24},{20,28},{24,16},{28,20},{1,9},{5... | collective-permute-start | bytes 98312 | tf_op jit(solution)/shard_map/ppermute | solution.py:401
  45.8 1.8 %collective-permute-start.12 = (bf16[64,256]{1,0:T(8,128)(2,1)S(1)}, bf16[64,256]{1,0:T(8,128)(2,1)S(1)}, u32[]{:S(2)}, u32[]{:S(2)}) collective-permute-start(bf16[64,256]{1,0:T(8,128)(2,1)S(1)} %finish_queries.1.refs_0_), channel_id=1, source_target_pairs={{0,16},{4,20},{8,24},{12,28},{16,0},{20,4},{24,8},{28,12},{1,17},{... | collective-permute-start | bytes 98312 | tf_op jit(solution)/shard_map/ppermute | solution.py:401
  47.6 0.0 collective-permute-done.10.refs_3_
  47.6 1.9 %collective-permute-start.13 = (bf16[64,256]{1,0:T(8,128)(2,1)S(1)}, bf16[64,256]{1,0:T(8,128)(2,1)S(1)}, u32[]{:S(2)}, u32[]{:S(2)}) collective-permute-start(bf16[64,256]{1,0:T(8,128)(2,1)S(1)} %finish_queries.1.refs_0_), channel_id=1, source_target_pairs={{0,24},{4,28},{8,16},{12,20},{16,8},{20,12},{24,0},{28,4},{1,25},{... | collective-permute-start | bytes 98312 | tf_op jit(solution)/shard_map/ppermute | solution.py:401
  49.5 0.0 collective-permute-done.8.refs_1_
  49.6 11.2 %context_attention.2.refs_4_ = bf16[1024,1024]{1,0:T(8,128)(2,1)} custom-call(s32[8]{0:T(128)S(1)} %copy-done.9, s32[8]{0:T(128)S(1)} %copy-done.10, bf16[1024,1024]{1,0:T(8,128)(2,1)S(1)} %copy-done.11, bf16[1024,128]{1,0:T(8,128)(2,1)S(1)} %copy-done.3, bf16[1024,128]{1,0:T(8,128)(2,1)S(1)} %copy-done.6, bf16[512,128]{1,0:T(8,128)(2,1)S(1)} %get-tuple-element.47.refs_0_, ...), custom_call_target="tpu_custom_call" | custom-call | flops 3221225472 | bytes 3145728 | tf_op jit(solution)/shard_map/context_attention/pallas_call | solution.py:119
  60.7 0.0 collective-permute-done.11.refs_1_
  60.7 0.0 collective-permute-done.12.refs_2_
  60.7 0.0 collective-permute-done.13.refs_3_
  60.8 0.5 project.1
  61.3 0.1 collective-permute-start.14
  61.4 1.6 %collective-permute-start.15 = (f32[16,1024]{1,0:T(8,128)S(1)}, f32[16,1024]{1,0:T(8,128)S(1)}, u32[]{:S(2)}, u32[]{:S(2)}) collective-permute-start(f32[16,1024]{1,0:T(8,128)S(1)} %get-tuple-element.50), channel_id=1, source_target_pairs={{0,2},{1,3},{2,0},{3,1},{4,6},{5,7},{6,4},{7,5},{8,10},{9,11},{10,... | collective-permute-start | bytes 196616 | tf_op jit(solution)/shard_map/ppermute | solution.py:401
  62.9 0.3 collective-permute-start.16
  63.2 11.2 %context_attention.3 = bf16[1024,1024]{1,0:T(8,128)(2,1)} custom-call(s32[8]{0:T(128)S(1)} %copy-done.9, s32[8]{0:T(128)S(1)} %copy-done.10, bf16[1024,1024]{1,0:T(8,128)(2,1)S(1)} %copy-done.11, bf16[1024,128]{1,0:T(8,128)(2,1)S(1)} %copy-done.3, bf16[1024,128]{1,0:T(8,128)(2,1)S(1)} %copy-done.6, ...), custom_call_target="tpu_custom_call", output_to_operand_aliasing={{}: (9, {})} | custom-call | flops 3221225472 | bytes 3145728 | tf_op jit(solution)/shard_map/context_attention/pallas_call | solution.py:119
  74.4 0.6 add_convert_fusion
  (21 shorter events, 0.1 us)
Async XLA Ops:
  0.6 1.0 %copy-start.1 = (bf16[1024,128]{1,0:T(8,128)(2,1)S(1)}, bf16[1024,128]{1,0:T(8,128)(2,1)}, u32[]{:S(2)}) copy-start(bf16[1024,128]{1,0:T(8,128)(2,1)} %k_ref.6) | copy-start | bytes 786436
  1.6 0.9 %copy-start.4 = (bf16[1024,128]{1,0:T(8,128)(2,1)S(1)}, bf16[1024,128]{1,0:T(8,128)(2,1)}, u32[]{:S(2)}) copy-start(bf16[1024,128]{1,0:T(8,128)(2,1)} %v_ref.6) | copy-start | bytes 786436
  2.5 0.7 copy-start.7
  3.3 24.5 %copy-start.10 = (s32[8]{0:T(128)S(1)}, s32[8]{0:T(128)}, u32[]{:S(2)}) copy-start(s32[8]{0:T(128)} %lens.5) | copy-start | bytes 100
  3.3 46.3 %copy-start.3 = (bf16[1024,128]{1,0:T(8,128)(2,1)S(1)}, bf16[1024,128]{1,0:T(8,128)(2,1)}, u32[]{:S(2)}) copy-start(bf16[1024,128]{1,0:T(8,128)(2,1)} %k_ref.6) | copy-start | bytes 786436
  3.3 46.3 %copy-start.6 = (bf16[1024,128]{1,0:T(8,128)(2,1)S(1)}, bf16[1024,128]{1,0:T(8,128)(2,1)}, u32[]{:S(2)}) copy-start(bf16[1024,128]{1,0:T(8,128)(2,1)} %v_ref.6) | copy-start | bytes 786436
  3.3 46.3 %copy-start.9 = (s32[8]{0:T(128)S(1)}, s32[8]{0:T(128)}, u32[]{:S(2)}) copy-start(s32[8]{0:T(128)} %blocks.3) | copy-start | bytes 100
  3.3 7.5 %collective-permute-start = (bf16[576,128]{1,0:T(8,128)(2,1)S(1)}, bf16[576,128]{1,0:T(8,128)(2,1)S(1)}, u32[]{:S(2)}, u32[]{:S(2)}) collective-permute-start(bf16[576,128]{1,0:T(8,128)(2,1)S(1)} %get-tuple-element.33), channel_id=1, source_target_pairs={{0,4},{4,0},{8,12},{12,8},{16,20},{20,16},{24,28},{28,24},{1,5},{5... | collective-permute-start | bytes 442376 | tf_op jit(solution)/shard_map/ppermute | solution.py:401
  6.4 6.8 %collective-permute-start.1 = (bf16[576,128]{1,0:T(8,128)(2,1)S(1)}, bf16[576,128]{1,0:T(8,128)(2,1)S(1)}, u32[]{:S(2)}, u32[]{:S(2)}) collective-permute-start(bf16[576,128]{1,0:T(8,128)(2,1)S(1)} %get-tuple-element.34), channel_id=1, source_target_pairs={{0,8},{4,12},{8,0},{12,4},{16,24},{20,28},{24,16},{28,20},{1,9},{5... | collective-permute-start | bytes 442376 | tf_op jit(solution)/shard_map/ppermute | solution.py:401
  7.9 6.7 %collective-permute-start.2 = (bf16[576,128]{1,0:T(8,128)(2,1)S(1)}, bf16[576,128]{1,0:T(8,128)(2,1)S(1)}, u32[]{:S(2)}, u32[]{:S(2)}) collective-permute-start(bf16[576,128]{1,0:T(8,128)(2,1)S(1)} %get-tuple-element.35), channel_id=1, source_target_pairs={{0,12},{4,8},{8,4},{12,0},{16,28},{20,24},{24,20},{28,16},{1,13},{... | collective-permute-start | bytes 442376 | tf_op jit(solution)/shard_map/ppermute | solution.py:401
  7.9 1.0 %copy-start.2 = (bf16[1024,128]{1,0:T(8,128)(2,1)S(1)}, bf16[1024,128]{1,0:T(8,128)(2,1)}, u32[]{:S(2)}) copy-start(bf16[1024,128]{1,0:T(8,128)(2,1)} %k_ref.6) | copy-start | bytes 786436
  8.9 0.9 %copy-start.5 = (bf16[1024,128]{1,0:T(8,128)(2,1)S(1)}, bf16[1024,128]{1,0:T(8,128)(2,1)}, u32[]{:S(2)}) copy-start(bf16[1024,128]{1,0:T(8,128)(2,1)} %v_ref.6) | copy-start | bytes 786436
  14.6 0.7 copy-start.8
  15.3 34.3 %copy-start.11 = (bf16[1024,1024]{1,0:T(8,128)(2,1)S(1)}, bf16[1024,1024]{1,0:T(8,128)(2,1)}, u32[]{:S(2)}) copy-start(bf16[1024,1024]{1,0:T(8,128)(2,1)} %q_ref.5) | copy-start | bytes 6291460
  15.9 11.3 %collective-permute-start.3 = (bf16[768,128]{1,0:T(8,128)(2,1)S(1)}, bf16[768,128]{1,0:T(8,128)(2,1)S(1)}, u32[]{:S(2)}, u32[]{:S(2)}) collective-permute-start(bf16[768,128]{1,0:T(8,128)(2,1)S(1)} %regroup.1.own), channel_id=1, source_target_pairs={{0,16},{4,20},{8,24},{12,28},{16,0},{20,4},{24,8},{28,12},{1,17},{... | collective-permute-start | bytes 589832 | tf_op jit(solution)/shard_map/ppermute | solution.py:401
  30.0 5.8 %collective-permute-start.4 = (f32[136,128]{1,0:T(8,128)S(1)}, f32[136,128]{1,0:T(8,128)S(1)}, u32[]{:S(2)}, u32[]{:S(2)}) collective-permute-start(f32[136,128]{1,0:T(8,128)S(1)} %get-tuple-element.41), channel_id=1, source_target_pairs={{0,8},{4,12},{8,0},{12,4},{16,24},{20,28},{24,16},{28,20},{1,9},{5... | collective-permute-start | bytes 208904 | tf_op jit(solution)/shard_map/ppermute | solution.py:401
  30.4 8.0 %collective-permute-start.5 = (f32[136,128]{1,0:T(8,128)S(1)}, f32[136,128]{1,0:T(8,128)S(1)}, u32[]{:S(2)}, u32[]{:S(2)}) collective-permute-start(f32[136,128]{1,0:T(8,128)S(1)} %get-tuple-element.42), channel_id=1, source_target_pairs={{0,16},{4,20},{8,24},{12,28},{16,0},{20,4},{24,8},{28,12},{1,17},{... | collective-permute-start | bytes 208904 | tf_op jit(solution)/shard_map/ppermute | solution.py:401
  33.8 6.5 %collective-permute-start.6 = (f32[136,128]{1,0:T(8,128)S(1)}, f32[136,128]{1,0:T(8,128)S(1)}, u32[]{:S(2)}, u32[]{:S(2)}) collective-permute-start(f32[136,128]{1,0:T(8,128)S(1)} %get-tuple-element.43), channel_id=1, source_target_pairs={{0,24},{4,28},{8,16},{12,20},{16,8},{20,12},{24,0},{28,4},{1,25},{... | collective-permute-start | bytes 208904 | tf_op jit(solution)/shard_map/ppermute | solution.py:401
  34.5 13.1 %collective-permute-start.10 = (bf16[512,128]{1,0:T(8,128)(2,1)S(1)}, bf16[512,128]{1,0:T(8,128)(2,1)S(1)}, u32[]{:S(2)}, u32[]{:S(2)}) collective-permute-start(bf16[512,128]{1,0:T(8,128)(2,1)S(1)} %get-tuple-element.47.refs_0_), channel_id=1, source_target_pairs={{0,12},{4,8},{8,4},{12,0},{16,28},{20,24},{24,20},{28,16},{1,13},{... | collective-permute-start | bytes 393224 | tf_op jit(solution)/shard_map/ppermute | solution.py:401
  35.2 14.4 %collective-permute-start.8 = (bf16[512,128]{1,0:T(8,128)(2,1)S(1)}, bf16[512,128]{1,0:T(8,128)(2,1)S(1)}, u32[]{:S(2)}, u32[]{:S(2)}) collective-permute-start(bf16[512,128]{1,0:T(8,128)(2,1)S(1)} %get-tuple-element.47.refs_0_), channel_id=1, source_target_pairs={{0,4},{4,0},{8,12},{12,8},{16,20},{20,16},{24,28},{28,24},{1,5},{5... | collective-permute-start | bytes 393224 | tf_op jit(solution)/shard_map/ppermute | solution.py:401
  35.8 13.7 %collective-permute-start.9 = (bf16[512,128]{1,0:T(8,128)(2,1)S(1)}, bf16[512,128]{1,0:T(8,128)(2,1)S(1)}, u32[]{:S(2)}, u32[]{:S(2)}) collective-permute-start(bf16[512,128]{1,0:T(8,128)(2,1)S(1)} %get-tuple-element.47.refs_0_), channel_id=1, source_target_pairs={{0,8},{4,12},{8,0},{12,4},{16,24},{20,28},{24,16},{28,20},{1,9},{5... | collective-permute-start | bytes 393224 | tf_op jit(solution)/shard_map/ppermute | solution.py:401
  40.3 4.4 %collective-permute-start.7 = (f32[136,128]{1,0:T(8,128)S(1)}, f32[136,128]{1,0:T(8,128)S(1)}, u32[]{:S(2)}, u32[]{:S(2)}) collective-permute-start(f32[136,128]{1,0:T(8,128)S(1)} %merge_partials.1.refs_0_), channel_id=1, source_target_pairs={{0,4},{4,0},{8,12},{12,8},{16,20},{20,16},{24,28},{28,24},{1,5},{5... | collective-permute-start | bytes 208904 | tf_op jit(solution)/shard_map/ppermute | solution.py:401
  45.1 15.7 %copy-start = (bf16[1024,1024]{1,0:T(8,128)(2,1)S(1)}, bf16[1024,1024]{1,0:T(8,128)(2,1)}, u32[]{:S(2)}) copy-start(bf16[1024,1024]{1,0:T(8,128)(2,1)} %refs_4_.1) | copy-start | bytes 6291460
  45.1 15.7 %collective-permute-start.11 = (bf16[64,256]{1,0:T(8,128)(2,1)S(1)}, bf16[64,256]{1,0:T(8,128)(2,1)S(1)}, u32[]{:S(2)}, u32[]{:S(2)}) collective-permute-start(bf16[64,256]{1,0:T(8,128)(2,1)S(1)} %finish_queries.1.refs_0_), channel_id=1, source_target_pairs={{0,8},{4,12},{8,0},{12,4},{16,24},{20,28},{24,16},{28,20},{1,9},{5... | collective-permute-start | bytes 98312 | tf_op jit(solution)/shard_map/ppermute | solution.py:401
  45.8 14.9 %collective-permute-start.12 = (bf16[64,256]{1,0:T(8,128)(2,1)S(1)}, bf16[64,256]{1,0:T(8,128)(2,1)S(1)}, u32[]{:S(2)}, u32[]{:S(2)}) collective-permute-start(bf16[64,256]{1,0:T(8,128)(2,1)S(1)} %finish_queries.1.refs_0_), channel_id=1, source_target_pairs={{0,16},{4,20},{8,24},{12,28},{16,0},{20,4},{24,8},{28,12},{1,17},{... | collective-permute-start | bytes 98312 | tf_op jit(solution)/shard_map/ppermute | solution.py:401
  47.6 13.2 %collective-permute-start.13 = (bf16[64,256]{1,0:T(8,128)(2,1)S(1)}, bf16[64,256]{1,0:T(8,128)(2,1)S(1)}, u32[]{:S(2)}, u32[]{:S(2)}) collective-permute-start(bf16[64,256]{1,0:T(8,128)(2,1)S(1)} %finish_queries.1.refs_0_), channel_id=1, source_target_pairs={{0,24},{4,28},{8,16},{12,20},{16,8},{20,12},{24,0},{28,4},{1,25},{... | collective-permute-start | bytes 98312 | tf_op jit(solution)/shard_map/ppermute | solution.py:401
  61.3 13.1 %collective-permute-start.14 = (f32[16,1024]{1,0:T(8,128)S(1)}, f32[16,1024]{1,0:T(8,128)S(1)}, u32[]{:S(2)}, u32[]{:S(2)}) collective-permute-start(f32[16,1024]{1,0:T(8,128)S(1)} %get-tuple-element.49), channel_id=1, source_target_pairs={{0,1},{1,0},{2,3},{3,2},{4,5},{5,4},{6,7},{7,6},{8,9},{9,8},{10,11... | collective-permute-start | bytes 196616 | tf_op jit(solution)/shard_map/ppermute | solution.py:401
  61.4 13.1 %collective-permute-start.15 = (f32[16,1024]{1,0:T(8,128)S(1)}, f32[16,1024]{1,0:T(8,128)S(1)}, u32[]{:S(2)}, u32[]{:S(2)}) collective-permute-start(f32[16,1024]{1,0:T(8,128)S(1)} %get-tuple-element.50), channel_id=1, source_target_pairs={{0,2},{1,3},{2,0},{3,1},{4,6},{5,7},{6,4},{7,5},{8,10},{9,11},{10,... | collective-permute-start | bytes 196616 | tf_op jit(solution)/shard_map/ppermute | solution.py:401
  62.9 11.5 %collective-permute-start.16 = (f32[16,1024]{1,0:T(8,128)S(1)}, f32[16,1024]{1,0:T(8,128)S(1)}, u32[]{:S(2)}, u32[]{:S(2)}) collective-permute-start(f32[16,1024]{1,0:T(8,128)S(1)} %get-tuple-element.51), channel_id=1, source_target_pairs={{0,3},{1,2},{2,1},{3,0},{4,7},{5,6},{6,5},{7,4},{8,11},{9,10},{10,... | collective-permute-start | bytes 196616 | tf_op jit(solution)/shard_map/ppermute | solution.py:401
